TPU v7x, 512 devices: a whole 4x4x16 slice. The times are simulated.
512 devices in a mesh: seq: 32 (over z, y_lo), mp: 16 (over x, y_hi, core).
Axes of the slice: x: 4, y: 4 (y_hi: 2, y_lo: 2; y = y_hi * 2 + y_lo), z: 16, core: 2. Of those that a mesh axis runs over, the one named last changes fastest.
Arguments:
- queries: bfloat16 [16384, 8192], P('seq', 'mp'), may hold values from -6 to 6
- keys_in: bfloat16 [16384, 8192], P('seq', 'mp'), may hold values from -6 to 6
- values_in: bfloat16 [16384, 8192], P('seq', 'mp'), may hold values from -6 to 6
- residual: bfloat16 [16384, 8192], P('seq', 'mp')
- short_taps: bfloat16 [3, 7, 8192], P(None, None, 'mp'), may hold values from -2 to 2
- mr_filter: bfloat16 [128, 512], P('seq', 'mp'), may hold values from -0.5 to 0.5
- norm_gain: bfloat16 [8192], P('mp'), may hold values from 0.5 to 1.5
- predecessor: int32 [32], replicated, may hold values from -1 to 31, as said below
- stretch_lengths: int32 [32], replicated, may hold values from 1 to 512, as said below
Outputs:
- mixed: bfloat16 [16384, 8192], P('seq', 'mp')
- normed: bfloat16 [16384, 8192], P('seq', 'mp')
Inputs may be any that keep to these rules, and one draw needn't show every extreme that they name: predecessor[j] is the stretch holding the preceding 512 tokens of stretch j's genome, or -1 for a genome's first stretch; each stretch precedes at most one stretch, and the chains have no cycles. `stretch_lengths`: every stretch that precedes another stretch is full (512 valid tokens); valid tokens come first.
All inputs are finite; a program needn't handle non-finite values.
Results may differ from a plain program's by a relative error of at most 0.0049.
Values may be sent and summed in bfloat16 or wider, within the bound.
A program may use at most 64 MiB of HBM per device.

v0:
```python
import jax
import jax.numpy as jnp
from jax import lax
from jax.sharding import PartitionSpec as P

EPSILON = 1e-06


def featurize(extended, taps):
    length = extended.shape[0] - 8
    total = jnp.zeros((length, extended.shape[1]), jnp.float32)
    for offset in range(taps.shape[0]):
        total = total + taps[offset].astype(jnp.float32) * extended[
            8 - offset : 8 - offset + length
        ].astype(jnp.float32)
    return total


def toeplitz_blocks(filter_rows):
    tap_count = filter_rows.shape[0]
    group_count = filter_rows.shape[1]
    flipped = filter_rows[::-1].T
    pattern = jnp.concatenate(
        [
            jnp.zeros((group_count, 1), filter_rows.dtype),
            flipped,
            jnp.zeros((group_count, tap_count), filter_rows.dtype),
        ],
        axis=1,
    )
    tiled = jnp.tile(pattern, (1, tap_count))[:, : 2 * tap_count * tap_count]
    return tiled.reshape(group_count, tap_count, 2 * tap_count)


def long_conv(extended, filter_rows, group_size):
    tap_count = filter_rows.shape[0]
    length = extended.shape[0] - tap_count
    blocks = length // tap_count
    channels = extended.shape[1]
    pieces = extended.reshape(blocks + 1, tap_count, channels)
    windows = jnp.concatenate([pieces[:-1], pieces[1:]], axis=1).reshape(
        blocks, 2 * tap_count, channels // group_size, group_size
    )
    matrices = toeplitz_blocks(filter_rows)
    result = jnp.einsum("gij,bjgc->bigc", matrices, windows, preferred_element_type=jnp.float32)
    return result.reshape(length, channels)


def body(
    queries,
    keys_in,
    values_in,
    residual,
    short_taps,
    mr_filter,
    norm_gain,
    predecessor,
    stretch_lengths,
):
    row_count, width = queries.shape
    device = lax.axis_index("seq")
    filter_rows = lax.all_gather(mr_filter, "seq", axis=0, tiled=True)
    tap_count = filter_rows.shape[0]
    group_size = width // filter_rows.shape[1]
    blank = jnp.zeros((8, width), queries.dtype)
    key_feat = featurize(jnp.concatenate([blank, keys_in]), short_taps[1])
    value_feat = featurize(jnp.concatenate([blank, values_in]), short_taps[2])
    mixed_in = (key_feat * value_feat).astype(jnp.bfloat16)
    state_tail = mixed_in[row_count - tap_count :][None]
    raw_tail = jnp.concatenate(
        [queries[row_count - 8 :], keys_in[row_count - 8 :], values_in[row_count - 8 :]], axis=1
    )[None]
    source = predecessor[device]
    carry = (jnp.zeros_like(state_tail), jnp.zeros_like(raw_tail))
    piece = (
        lax.all_gather(state_tail, "seq", axis=0, tiled=True),
        lax.all_gather(raw_tail, "seq", axis=0, tiled=True),
    )
    count = piece[0].shape[0]
    inside = (source >= 0) & (source < count)
    offset = jnp.clip(source, 0, count - 1)
    prev_state, prev_raw = tuple(
        (
            jnp.where(inside, lax.dynamic_slice_in_dim(member, offset, 1, 0), kept)
            for member, kept in zip(piece, carry)
        )
    )
    prev_rows = prev_raw[0]
    prev_query = prev_rows[:, :width]
    prev_key = prev_rows[:, width : 2 * width]
    prev_value = prev_rows[:, 2 * width :]
    query_feat = featurize(jnp.concatenate([prev_query, queries]), short_taps[0])
    head_key = featurize(jnp.concatenate([prev_key, keys_in[:8]]), short_taps[1])
    head_value = featurize(jnp.concatenate([prev_value, values_in[:8]]), short_taps[2])
    head_mixed = (head_key * head_value).astype(jnp.bfloat16)
    mixed_in = jnp.concatenate([head_mixed, mixed_in[8:]])
    extended = jnp.concatenate([prev_state[0], mixed_in])
    filtered = long_conv(extended, filter_rows, group_size)
    valid = (jnp.arange(row_count, dtype=jnp.int32) < stretch_lengths[device])[:, None]
    mixed = jnp.where(valid, query_feat * filtered, 0.0).astype(jnp.bfloat16)
    summed = residual.astype(jnp.float32) + mixed.astype(jnp.float32)
    squares_total = lax.psum(jnp.sum(summed * summed, axis=1), "mp")
    scale_rows = lax.rsqrt(squares_total / (width * lax.axis_size("mp")) + EPSILON)
    normed = jnp.where(
        valid, summed * scale_rows[:, None] * norm_gain.astype(jnp.float32), 0.0
    ).astype(jnp.bfloat16)
    return (mixed, normed)


def solution(mesh):
    in_specs = (
        P("seq", "mp"),
        P("seq", "mp"),
        P("seq", "mp"),
        P("seq", "mp"),
        P(None, None, "mp"),
        P("seq", "mp"),
        P("mp"),
        P(),
        P(),
    )
    out_specs = (P("seq", "mp"), P("seq", "mp"))
    return jax.shard_map(body, mesh=mesh, in_specs=in_specs, out_specs=out_specs, check_vma=False)
```

profile of v0, /device:TPU:1, one launch (start us, length us, event | category | flops | bytes accessed | tf_op | source)
XLA Modules:
  0.0 226.0 jit_solution(18346637916515088260)
XLA Ops:
  7.2 1.0 slice_convert_fusion.20
  8.2 0.8 slice_convert_fusion.1
  9.0 5.3 %multiply_convert_fusion = bf16[512,512]{1,0:T(8,128)(2,1)S(1)} fusion(bf16[512,512]{1,0:T(8,128)(2,1)} %param.11, bf16[512,512]{1,0:T(8,128)(2,1)} %param.10, f32[512]{0:T(512)S(1)} %bitcast.92, f32[512]{0:T(512)S(1)} %bitcast.90, f32[512]{0:T(512)S(1)} %bitcast.66, f32[512]{0:T(512)S(1)} %bitcast.68, f32[512]{0:T(512)S(1)} %bitcast.70, ...), kind=kLoop, calls=%fused_computation.17 | loop fusion | flops 11010048 | bytes 1601536 | tf_op jit(solution)/shard_map/convert_element_type | solution.py:68
  14.4 0.7 slice.328
  16.9 1.0 copy.66
  18.5 56.7 %all-gather.2 = bf16[32,4,32]{2,1,0:T(4,128)(2,1)S(1)} all-gather(bf16[1,4,32]{2,1,0:T(4,128)(2,1)S(1)} %bitcast.102), channel_id=1, replica_groups=mesh['seq'=32,'mp'=16] {'seq'}, dimensions={0}, use_global_device_ids=true | all-gather | bytes 8448 | tf_op jit(solution)/shard_map/all_gather | solution.py:62
  75.8 4.4 %tile.10 = bf16[32,32896]{1,0:T(8,128)(2,1)} reshape(bf16[32,128,257]{2,1,0:T(8,128)(2,1)S(1)} %tile.4) | data formatting | bytes 4210688 | tf_op jit(solution)/shard_map/tile | solution.py:31
  80.3 1.6 slice-done
  82.4 0.8 fusion.27
  83.2 59.5 %all-gather = bf16[256,1536]{1,0:T(8,128)(2,1)S(1)} all-gather(bf16[8,1536]{1,0:T(8,128)(2,1)S(1)} %pad_maximum_fusion.4), channel_id=2, replica_groups=mesh['seq'=32,'mp'=16] {'seq'}, dimensions={0}, use_global_device_ids=true | all-gather | bytes 811008 | tf_op jit(solution)/shard_map/all_gather | solution.py:77
  143.6 1.3 copy.75
  145.7 4.9 %all-gather.5.cloned.1.call-done = bf16[4096,512]{1,0:T(8,128)(2,1)} async-done(((bf16[128,512]{1,0:T(8,128)(2,1)}), bf16[4096,512]{1,0:T(8,128)(2,1)}) %all-gather.5.cloned.1.call-update) | async-done | bytes 4194320 | tf_op jit(solution)/shard_map/all_gather | solution.py:76
  150.6 0.9 select_bitcast_fusion
  151.5 1.0 pad_maximum_fusion
  152.6 2.1 copy.69
  154.7 2.0 concatenate.42
  156.7 1.9 copy.71
  158.6 1.0 copy.70
  159.6 1.2 concatenate.44
  160.9 1.9 fusion.2
  163.8 2.1 multiply_reduce_fusion
  165.9 51.0 %psum.7 = f32[512]{0:T(512)S(1)} all-reduce(f32[512]{0:T(512)S(1)} %get-tuple-element.8), channel_id=1, replica_groups=mesh['seq'=32,'mp'=16] {'mp'}, use_global_device_ids=true, to_apply=%region_1.2 | all-reduce | flops 512 | bytes 4096 | tf_op jit(solution)/shard_map/psum | solution.py:102
  216.9 1.0 copy.76
  218.1 1.0 copy.77
  (44 shorter events, 4.8 us)
Async XLA Ops:
  7.2 8.0 %copy-start.6 = (s32[32]{0:T(128)S(1)}, s32[32]{0:T(128)}, u32[]{:S(2)}) copy-start(s32[32]{0:T(128)} %param.16) | copy-start | bytes 388
  7.2 9.7 %copy-start.3 = (bf16[512,512]{1,0:T(8,128)(2,1)S(1)}, bf16[512,512]{1,0:T(8,128)(2,1)}, u32[]{:S(2)}) copy-start(bf16[512,512]{1,0:T(8,128)(2,1)} %param.9) | copy-start | bytes 1572868
  7.2 143.4 %all-gather.5.cloned.1.call-start = ((), (), s32[]{:S(2)}) async-start(), calls=%async_computation | async-start | bytes 4325376 | tf_op jit(solution)/shard_map/all_gather | solution.py:76
  8.2 10.2 %copy-start.4 = (bf16[4,32]{1,0:T(4,128)(2,1)S(1)}, bf16[4,32]{1,0:T(4,128)(2,1)}, u32[]{:S(2)}) copy-start(bf16[4,32]{1,0:T(4,128)(2,1)} %param.14) | copy-start | bytes 772
  14.4 61.1 %copy-start = (bf16[512,512]{1,0:T(8,128)(2,1)}, bf16[512,512]{1,0:T(8,128)(2,1)S(1)}, u32[]{:S(2)}) copy-start(bf16[512,512]{1,0:T(8,128)(2,1)S(1)} %multiply_convert_fusion) | copy-start | bytes 1572868
  80.3 1.6 slice-start
  81.9 1.3 slice-start.2
  81.9 61.1 %copy-start.7 = (s32[32]{0:T(128)S(1)}, s32[32]{0:T(128)}, u32[]{:S(2)}) copy-start(s32[32]{0:T(128)} %param.17) | copy-start | bytes 388
  82.4 62.5 %copy-start.5 = (bf16[512]{0:T(512)(128)(2,1)S(1)}, bf16[512]{0:T(512)(128)(2,1)}, u32[]{:S(2)}) copy-start(bf16[512]{0:T(512)(128)(2,1)} %param.15) | copy-start | bytes 3076
  82.4 69.1 %slice-start.1 = ((bf16[512,512]{1,0:T(8,128)(2,1)}), bf16[504,512]{1,0:T(8,128)(2,1)S(1)}, s32[]{:S(2)}) async-start(bf16[512,512]{1,0:T(8,128)(2,1)} %copy-done), calls=%async_computation.2 | async-start | bytes 1032192 | tf_op jit(solution)/shard_map/slice | solution.py:96
  152.6 6.0 %copy-start.1 = (bf16[512,512]{1,0:T(8,128)(2,1)S(1)}, bf16[512,512]{1,0:T(8,128)(2,1)}, u32[]{:S(2)}) copy-start(bf16[512,512]{1,0:T(8,128)(2,1)} %get-tuple-element.11) | copy-start | bytes 1572868
  162.8 1.0 copy-start.2
Sparse Core Ops, SparseCore 0:
  15.3 135.2 all-gather.4
where the time goes:
time: 227 us; the launch traced here: 226 us
  blocking collectives  167 us (74%)
  local copies, waits for them, and re-layouts  23.7 us (10%)
  between operations  16 us (7%)
  other arithmetic  12.3 us (5%)
  waiting for transfers between devices  4.95 us (2%)
    all_gather x1, blocking collectives, body(): lax.all_gather(raw_tail, 'seq', axis=0, tiled=True)  59.5 us
    all_gather x1, blocking collectives, body(): filter_rows = lax.all_gather(mr_filter, 'seq', axis=0, tiled=True)  56.7 us
    psum x1, blocking collectives, body(): squares_total = lax.psum(jnp.sum(summed * summed, axis=1), 'mp')  51 us
    unnamed x22, local copies, waits for them, and re-layouts  5.46 us
    convert_element_type x1, other arithmetic, body(): mixed_in = (key_feat * value_feat).astype(jnp.bfloat16)  5.34 us
    concatenate x4, local copies, waits for them, and re-layouts, long_conv(): jnp.concatenate([pieces[:-1], pieces[1:]], axis=1)  5.16 us
    all_gather x1, waiting for transfers between devices, body(): lax.all_gather(state_tail, 'seq', axis=0, tiled=True)  4.93 us
    another operation x2, local copies, waits for them, and re-layouts, toeplitz_blocks(): tiled = jnp.tile(pattern, (1, tap_count))[:, :2 * tap_count * tap_count]  4.73 us
  transfers between devices with their start and end apart: 1, of which 1 were waited for; matrix products, arithmetic and copies ran while one was open for 5% of the time, Pallas kernels for 0%

commit v1 on v0

--- a/solution.py
+++ b/solution.py
@@ -74,7 +74,9 @@
     carry = (jnp.zeros_like(state_tail), jnp.zeros_like(raw_tail))
     piece = (
         lax.all_gather(state_tail, "seq", axis=0, tiled=True),
-        lax.all_gather(raw_tail, "seq", axis=0, tiled=True),
+        jnp.concatenate(
+            lax.all_to_all(jnp.stack([raw_tail] * lax.axis_size("seq")), "seq", 0, 0), axis=0
+        ),
     )
     count = piece[0].shape[0]
     inside = (source >= 0) & (source < count)

time: 227 us -> 238 us (1.048)
  blocking collectives: 167 us -> 131 us
  waiting for transfers between devices: 4.95 us -> 28.7 us
  starting transfers between devices: 0.04 us -> 17.2 us
  local copies, waits for them, and re-layouts: 23.7 us -> 26.3 us
  other arithmetic: 12.3 us -> 14.8 us
    all_gather x1 -> x0, blocking collectives: 59.5 us -> none  [body(): lax.all_gather(raw_tail, 'seq', axis=0, tiled=True)]
    all_gather x1, blocking collectives: 56.7 us -> 81.8 us  [body(): filter_rows = lax.all_gather(mr_filter, 'seq', axis=0, tiled=True)]
    all_gather x1, waiting for transfers between devices: 4.93 us -> 28.7 us  [body(): lax.all_gather(state_tail, 'seq', axis=0, tiled=True)]
    all_to_all x0 -> x1, starting transfers between devices: none -> 17.2 us  [body(): lax.all_to_all(jnp.stack([raw_tail] * lax.axis_size('seq')), 'seq', 0, 0)]
    unnamed x22 -> x69, local copies, waits for them, and re-layouts: 5.46 us -> 5.89 us
  transfers between devices with their start and end apart: 1 -> 2, of which waited for: 1 -> 1; matrix products, arithmetic and copies ran while one was open for 5% -> 7% of each run, Pallas kernels for 0% -> 0%
where the time goes in v1:
time: 238 us; the launch traced here: 237 us
  blocking collectives  131 us (55%)
  waiting for transfers between devices  28.7 us (12%)
  local copies, waits for them, and re-layouts  26.3 us (11%)
  starting transfers between devices  17.2 us (7%)
  between operations  16.6 us (7%)
  other arithmetic  14.8 us (6%)
    all_gather x1, blocking collectives, body(): filter_rows = lax.all_gather(mr_filter, 'seq', axis=0, tiled=True)  81.8 us
    psum x1, blocking collectives, body(): squares_total = lax.psum(jnp.sum(summed * summed, axis=1), 'mp')  49.5 us
    all_gather x1, waiting for transfers between devices, body(): lax.all_gather(state_tail, 'seq', axis=0, tiled=True)  28.7 us
    all_to_all x1, starting transfers between devices, body(): lax.all_to_all(jnp.stack([raw_tail] * lax.axis_size('seq')), 'seq', 0, 0)  17.2 us
    unnamed x69, local copies, waits for them, and re-layouts  5.89 us
    convert_element_type x1, other arithmetic, body(): mixed_in = (key_feat * value_feat).astype(jnp.bfloat16)  5.19 us
    concatenate x4, local copies, waits for them, and re-layouts, long_conv(): jnp.concatenate([pieces[:-1], pieces[1:]], axis=1)  5.13 us
  transfers between devices with their start and end apart: 2, of which 1 were waited for; matrix products, arithmetic and copies ran while one was open for 7% of the time, Pallas kernels for 0%

profile of v1, /device:TPU:1, one launch (start us, length us, event | category | flops | bytes accessed | tf_op | source)
XLA Modules:
  0.0 236.7 jit_solution(613467459014642783)
XLA Ops:
  7.2 1.6 slice_convert_fusion.20
  9.7 5.2 %multiply_convert_fusion = bf16[512,512]{1,0:T(8,128)(2,1)S(1)} fusion(bf16[512,512]{1,0:T(8,128)(2,1)} %param.11, bf16[512,512]{1,0:T(8,128)(2,1)} %param.10, f32[512]{0:T(512)S(1)} %bitcast.90, f32[512]{0:T(512)S(1)} %bitcast.88, f32[512]{0:T(512)S(1)} %bitcast.64, f32[512]{0:T(512)S(1)} %bitcast.66, f32[512]{0:T(512)S(1)} %bitcast.68, ...), kind=kLoop, calls=%fused_computation.17 | loop fusion | flops 11010048 | bytes 1601536 | tf_op jit(solution)/shard_map/convert_element_type | solution.py:68
  15.8 1.4 fusion.27
  17.2 1.0 stack.3
  18.1 17.2 %all-to-all-start = ((bf16[32,1,8,1536]{3,2,1,0:T(8,128)(2,1)}), bf16[32,1,8,1536]{3,2,1,0:T(8,128)(2,1)}, u32[]{:S(2)}, u32[]{:S(2)}) async-start(bf16[32,1,8,1536]{3,2,1,0:T(8,128)(2,1)} %stack.3), calls=%async_computation | async-start | bytes 1572864 | tf_op jit(solution)/shard_map/all_to_all | solution.py:78
  37.3 1.0 copy.55
  39.0 81.8 %all-gather.1 = bf16[32,4,32]{2,1,0:T(4,128)(2,1)S(1)} all-gather(bf16[1,4,32]{2,1,0:T(4,128)(2,1)S(1)} %bitcast.100), channel_id=1, replica_groups=mesh['seq'=32,'mp'=16] {'seq'}, dimensions={0}, use_global_device_ids=true | all-gather | bytes 8448 | tf_op jit(solution)/shard_map/all_gather | solution.py:62
  121.5 4.5 %tile.10 = bf16[32,32896]{1,0:T(8,128)(2,1)} reshape(bf16[32,128,257]{2,1,0:T(8,128)(2,1)S(1)} %tile.4) | data formatting | bytes 4210688 | tf_op jit(solution)/shard_map/tile | solution.py:31
  126.0 1.6 slice-done
  128.9 1.3 copy.66
  130.7 1.1 iota_compare_fusion
  133.1 1.1 multiply_convert_fusion.1
  134.2 28.7 %all-gather.4.cloned.1.call-done = bf16[4096,512]{1,0:T(8,128)(2,1)} async-done(((bf16[128,512]{1,0:T(8,128)(2,1)}), bf16[4096,512]{1,0:T(8,128)(2,1)}) %all-gather.4.cloned.1.call-update) | async-done | bytes 4194320 | tf_op jit(solution)/shard_map/all_gather | solution.py:76
  163.8 1.0 pad_maximum_fusion
  164.8 2.1 copy.60
  166.9 2.0 concatenate.42
  168.9 1.9 copy.62
  170.8 1.0 copy.61
  171.8 1.2 concatenate.44
  173.1 1.9 fusion.2
  176.1 2.1 multiply_reduce_fusion
  178.2 49.5 %psum.7 = f32[512]{0:T(512)S(1)} all-reduce(f32[512]{0:T(512)S(1)} %get-tuple-element.6), channel_id=1, replica_groups=mesh['seq'=32,'mp'=16] {'mp'}, use_global_device_ids=true, to_apply=%region_1.2 | all-reduce | flops 512 | bytes 4096 | tf_op jit(solution)/shard_map/psum | solution.py:104
  227.6 1.0 copy.67
  228.9 1.0 copy.68
  (95 shorter events, 8.2 us)
Async XLA Ops:
  7.2 10.0 %slice-start.2 = ((bf16[512,512]{1,0:T(8,128)(2,1)}), bf16[8,512]{1,0:T(8,128)(2,1)S(1)}, s32[]{:S(2)}) async-start(bf16[512,512]{1,0:T(8,128)(2,1)} %param.9), calls=%async_computation.4 | async-start | bytes 16384 | tf_op jit(solution)/shard_map/slice | solution.py:71
  7.2 155.6 %all-gather.4.cloned.1.call-start = ((), (), s32[]{:S(2)}) async-start(), calls=%async_computation.1 | async-start | bytes 4325376 | tf_op jit(solution)/shard_map/all_gather | solution.py:76
  8.8 6.1 %copy-start.5 = (f32[1,1,512]{2,1,0:T(1,128)}, f32[1,1,512]{2,1,0:T(1,128)S(1)}, u32[]{:S(2)}) copy-start(f32[1,1,512]{2,1,0:T(1,128)S(1)} %get-tuple-element.19) | copy-start | bytes 6148
  8.8 6.1 %copy-start.6 = (f32[1,1,512]{2,1,0:T(1,128)}, f32[1,1,512]{2,1,0:T(1,128)S(1)}, u32[]{:S(2)}) copy-start(f32[1,1,512]{2,1,0:T(1,128)S(1)} %get-tuple-element.20) | copy-start | bytes 6148
  8.8 6.1 %copy-start.7 = (f32[1,1,512]{2,1,0:T(1,128)}, f32[1,1,512]{2,1,0:T(1,128)S(1)}, u32[]{:S(2)}) copy-start(f32[1,1,512]{2,1,0:T(1,128)S(1)} %get-tuple-element.21) | copy-start | bytes 6148
  8.8 6.1 %copy-start.8 = (f32[1,1,512]{2,1,0:T(1,128)}, f32[1,1,512]{2,1,0:T(1,128)S(1)}, u32[]{:S(2)}) copy-start(f32[1,1,512]{2,1,0:T(1,128)S(1)} %get-tuple-element.22) | copy-start | bytes 6148
  8.9 6.1 %copy-start.9 = (f32[1,1,512]{2,1,0:T(1,128)}, f32[1,1,512]{2,1,0:T(1,128)S(1)}, u32[]{:S(2)}) copy-start(f32[1,1,512]{2,1,0:T(1,128)S(1)} %get-tuple-element.23) | copy-start | bytes 6148
  8.9 6.1 %copy-start.10 = (f32[1,1,512]{2,1,0:T(1,128)}, f32[1,1,512]{2,1,0:T(1,128)S(1)}, u32[]{:S(2)}) copy-start(f32[1,1,512]{2,1,0:T(1,128)S(1)} %get-tuple-element.24) | copy-start | bytes 6148
  8.9 6.1 %copy-start.11 = (f32[1,1,512]{2,1,0:T(1,128)}, f32[1,1,512]{2,1,0:T(1,128)S(1)}, u32[]{:S(2)}) copy-start(f32[1,1,512]{2,1,0:T(1,128)S(1)} %get-tuple-element.25) | copy-start | bytes 6148
  8.9 6.1 %copy-start.12 = (f32[1,1,512]{2,1,0:T(1,128)}, f32[1,1,512]{2,1,0:T(1,128)S(1)}, u32[]{:S(2)}) copy-start(f32[1,1,512]{2,1,0:T(1,128)S(1)} %get-tuple-element.26) | copy-start | bytes 6148
  8.9 6.1 %copy-start.13 = (f32[1,1,512]{2,1,0:T(1,128)}, f32[1,1,512]{2,1,0:T(1,128)S(1)}, u32[]{:S(2)}) copy-start(f32[1,1,512]{2,1,0:T(1,128)S(1)} %get-tuple-element.27) | copy-start | bytes 6148
  8.9 6.1 %copy-start.14 = (f32[1,1,512]{2,1,0:T(1,128)}, f32[1,1,512]{2,1,0:T(1,128)S(1)}, u32[]{:S(2)}) copy-start(f32[1,1,512]{2,1,0:T(1,128)S(1)} %get-tuple-element.28) | copy-start | bytes 6148
  8.9 6.1 %copy-start.15 = (f32[1,1,512]{2,1,0:T(1,128)}, f32[1,1,512]{2,1,0:T(1,128)S(1)}, u32[]{:S(2)}) copy-start(f32[1,1,512]{2,1,0:T(1,128)S(1)} %get-tuple-element.29) | copy-start | bytes 6148
  9.7 5.3 %copy-start.16 = (f32[1,1,512]{2,1,0:T(1,128)}, f32[1,1,512]{2,1,0:T(1,128)S(1)}, u32[]{:S(2)}) copy-start(f32[1,1,512]{2,1,0:T(1,128)S(1)} %get-tuple-element.36) | copy-start | bytes 6148
  9.7 5.3 %copy-start.17 = (f32[1,1,512]{2,1,0:T(1,128)}, f32[1,1,512]{2,1,0:T(1,128)S(1)}, u32[]{:S(2)}) copy-start(f32[1,1,512]{2,1,0:T(1,128)S(1)} %get-tuple-element.37) | copy-start | bytes 6148
  9.7 25.6 %copy-start.29 = (s32[32]{0:T(128)S(1)}, s32[32]{0:T(128)}, u32[]{:S(2)}) copy-start(s32[32]{0:T(128)} %param.16) | copy-start | bytes 388
  15.1 23.3 %copy-start = (bf16[512,512]{1,0:T(8,128)(2,1)}, bf16[512,512]{1,0:T(8,128)(2,1)S(1)}, u32[]{:S(2)}) copy-start(bf16[512,512]{1,0:T(8,128)(2,1)S(1)} %multiply_convert_fusion) | copy-start | bytes 1572868
  15.1 22.2 %copy-start.3 = (bf16[512,512]{1,0:T(8,128)(2,1)S(1)}, bf16[512,512]{1,0:T(8,128)(2,1)}, u32[]{:S(2)}) copy-start(bf16[512,512]{1,0:T(8,128)(2,1)} %param.9) | copy-start | bytes 1572868
  17.1 21.9 %copy-start.27 = (bf16[4,32]{1,0:T(4,128)(2,1)S(1)}, bf16[4,32]{1,0:T(4,128)(2,1)}, u32[]{:S(2)}) copy-start(bf16[4,32]{1,0:T(4,128)(2,1)} %param.14) | copy-start | bytes 772
  18.1 113.7 %all-to-all-start = ((bf16[32,1,8,1536]{3,2,1,0:T(8,128)(2,1)}), bf16[32,1,8,1536]{3,2,1,0:T(8,128)(2,1)}, u32[]{:S(2)}, u32[]{:S(2)}) async-start(bf16[32,1,8,1536]{3,2,1,0:T(8,128)(2,1)} %stack.3), calls=%async_computation | async-start | bytes 1572864 | tf_op jit(solution)/shard_map/all_to_all | solution.py:78
  127.6 2.6 %copy-start.28 = (bf16[512]{0:T(512)(128)(2,1)S(1)}, bf16[512]{0:T(512)(128)(2,1)}, u32[]{:S(2)}) copy-start(bf16[512]{0:T(512)(128)(2,1)} %param.15) | copy-start | bytes 3076
  128.2 35.5 %slice-start.1 = ((bf16[512,512]{1,0:T(8,128)(2,1)}), bf16[504,512]{1,0:T(8,128)(2,1)S(1)}, s32[]{:S(2)}) async-start(bf16[512,512]{1,0:T(8,128)(2,1)} %copy-done), calls=%async_computation.3 | async-start | bytes 1032192 | tf_op jit(solution)/shard_map/slice | solution.py:98
  164.8 6.0 %copy-start.1 = (bf16[512,512]{1,0:T(8,128)(2,1)S(1)}, bf16[512,512]{1,0:T(8,128)(2,1)}, u32[]{:S(2)}) copy-start(bf16[512,512]{1,0:T(8,128)(2,1)} %get-tuple-element.9) | copy-start | bytes 1572868
  175.5 53.2 %copy-start.25 = (f32[512]{0:T(512)S(1)}, f32[512]{0:T(512)}, u32[]{:S(2)}) copy-start(f32[512]{0:T(512)} %convert_element_type.432) | copy-start | bytes 6148
  (12 other events, 12.4 us)
Sparse Core Ops, SparseCore 0:
  15.9 146.8 all-gather.3
